TPU v7x, 128 devices: a whole 4x4x4 slice. The times are simulated.
128 devices in a mesh: fsdp: 16 (over z, x), ctx: 4 (over y_hi, core), tp: 2 (over y_lo).
Axes of the slice: x: 4, y: 4 (y_hi: 2, y_lo: 2; y = y_hi * 2 + y_lo), z: 4, core: 2. Of those that a mesh axis runs over, the one named last changes fastest.
Arguments:
- tokens: bfloat16 [16384, 2048], P(('fsdp', 'ctx')), may hold values from -6 to 6
- segments: int32 [16384], P(('fsdp', 'ctx')), may hold values from 0 to 2, as said below
- attn_gain: bfloat16 [2048], P('fsdp'), may hold values from 0.5 to 1.5
- q_weight: bfloat16 [2048, 2048], P('fsdp', 'tp'), may hold values from -0.125 to 0.125
- k_weight: bfloat16 [2048, 1024], P('fsdp', 'tp'), may hold values from -0.125 to 0.125
- v_weight: bfloat16 [2048, 1024], P('fsdp', 'tp'), may hold values from -0.125 to 0.125
- q_gain: bfloat16 [128], P('fsdp'), may hold values from 0.099609375 to 1.8984375
- k_gain: bfloat16 [128], P('fsdp'), may hold values from 0.099609375 to 1.8984375
- o_weight: bfloat16 [2048, 2048], P('tp', 'fsdp'), may hold values from -1.5 to 1.5
- mlp_gain: bfloat16 [2048], P('fsdp'), may hold values from 0.5 to 1.5
- gate_weight: bfloat16 [2048, 6144], P('fsdp', 'tp'), may hold values from -0.125 to 0.125
- up_weight: bfloat16 [2048, 6144], P('fsdp', 'tp'), may hold values from -0.125 to 0.125
- down_weight: bfloat16 [6144, 2048], P('tp', 'fsdp'), may hold values from -0.078125 to 0.078125
- cotangent: bfloat16 [16384, 2048], P(('fsdp', 'ctx')), may hold values from -6 to 6
Outputs:
- output: bfloat16 [16384, 2048], P(('fsdp', 'ctx'))
- grad_tokens: float32 [16384, 2048], P(('fsdp', 'ctx'))
- grad_attn_gain: float32 [2048], P('fsdp')
- grad_q_weight: float32 [2048, 2048], P('fsdp', 'tp')
- grad_k_weight: float32 [2048, 1024], P('fsdp', 'tp')
- grad_v_weight: float32 [2048, 1024], P('fsdp', 'tp')
- grad_q_gain: float32 [128], P('fsdp')
- grad_k_gain: float32 [128], P('fsdp')
- grad_o_weight: float32 [2048, 2048], P('tp', 'fsdp')
- grad_mlp_gain: float32 [2048], P('fsdp')
- grad_gate_weight: float32 [2048, 6144], P('fsdp', 'tp')
- grad_up_weight: float32 [2048, 6144], P('fsdp', 'tp')
- grad_down_weight: float32 [6144, 2048], P('tp', 'fsdp')
Inputs may be any that keep to these rules, and one draw needn't show every extreme that they name: `segments`: within each sequence of 1024 tokens the ids are 0, 1, 2 in three unbroken documents in that order; the middle one has 800 tokens and starts at a token from 64 to 160.
All inputs are finite; a program needn't handle non-finite values.
Results may differ from a plain program's by a relative error of at most 0.028.
Values may be sent and summed in bfloat16 or wider, within the bound.
A program may use at most 192 MiB of HBM per device.

v0:
```python
import jax
import jax.numpy as jnp
from jax import lax
from jax.experimental import pallas as pl
from jax.experimental.pallas import tpu as pltpu
from jax.sharding import PartitionSpec as P

HD = 128
MESH = pl.DeviceIdType.MESH
HBM = pl.BlockSpec(memory_space=pl.ANY)
VMEM = pl.BlockSpec(memory_space=pltpu.VMEM)
LOW = jnp.bfloat16
WIDE = jnp.float32
SCALE = HD ** (-0.5)


epsilon = 1e-06
rope_base = 1000000.0


def inverse_of(values_in):
    return lax.rsqrt(jnp.mean(values_in * values_in, -1, keepdims=True) + epsilon)


def norm_back(grad_in, unit_in, inverse):
    return inverse * (grad_in - unit_in * jnp.mean(grad_in * unit_in, -1, keepdims=True))


def dot_nn(left, right):
    return jnp.dot(left, right, preferred_element_type=WIDE)


def dot_tn(left, right):
    return lax.dot_general(left, right, (((0,), (0,)), ((), ())), preferred_element_type=WIDE)


def dot_nt(left, right):
    return lax.dot_general(left, right, (((1,), (1,)), ((), ())), preferred_element_type=WIDE)


def low(values_in):
    return values_in.astype(LOW)


def full(values_in):
    return values_in.astype(WIDE)


def place():
    plane = lax.axis_index("fsdp")
    part = lax.axis_index("ctx")
    half = lax.axis_index("tp")
    return {
        "z": lax.div(plane, 4),
        "x": lax.rem(plane, 4),
        "y": lax.div(part, 2) * 2 + half,
        "core": lax.rem(part, 2),
    }


def device(where):
    return (
        where["z"] * 4 + where["x"],
        lax.div(where["y"], 2) * 2 + where["core"],
        lax.rem(where["y"], 2),
    )


def moved(here, axis, step):
    there = dict(here)
    if axis == "pair":
        there["y"] = here["y"] + 1 - 2 * lax.rem(here["y"], 2)
    elif axis == "cross":
        there["y"] = 3 - here["y"]
    elif axis == "core":
        there["core"] = 1 - here["core"]
    else:
        there[axis] = lax.rem(here[axis] + step, 4)
    return there


def block_of(y, core):
    return lax.div(y, 2) * 4 + core * 2 + lax.rem(y, 2)


class Group:
    def __init__(self, copies):
        self.copies = copies

    def wait_recv(self):
        for copy in self.copies:
            copy.wait_recv()


class Links:
    def __init__(self, send_sems, recv_sems):
        self.here = place()
        self.send_sems, self.recv_sems = send_sems, recv_sems
        self.started = []

    def meet(self, peers):
        barrier = pltpu.get_barrier_semaphore()
        for axis, step in peers:
            pl.semaphore_signal(
                barrier,
                inc=1,
                device_id=device(moved(self.here, axis, step)),
                device_id_type=MESH,
            )
        pl.semaphore_wait(barrier, len(peers))

    def send(self, src, dst, axis, step=0):
        if isinstance(src, list):
            return Group([self.send(a, b, axis, step) for a, b in zip(src, dst)])
        spot = len(self.started)
        assert spot < self.send_sems.shape[0]
        copy = pltpu.make_async_remote_copy(
            src_ref=src,
            dst_ref=dst,
            send_sem=self.send_sems.at[spot],
            recv_sem=self.recv_sems.at[spot],
            device_id=device(moved(self.here, axis, step)),
            device_id_type=MESH,
        )
        copy.start()
        self.started.append(copy)
        return copy

    def drain(self):
        for copy in self.started:
            copy.wait_send()


class Locals:
    def __init__(self, sems):
        self.sems = sems
        self.count = 0

    def start(self, src, dst):
        assert self.count < self.sems.shape[0]
        copy = pltpu.make_async_copy(src, dst, self.sems.at[self.count])
        self.count += 1
        copy.start()
        return copy


PLANE = [("x", 1), ("x", 2), ("x", 3), ("z", 1), ("z", 2), ("z", 3)]
COLUMN = [("y", 1), ("y", 2), ("y", 3), ("core", 0)]


def step_all(jobs):
    left = []
    for job in jobs:
        try:
            next(job)
            left.append(job)
        except StopIteration:
            pass
    return left


def together(jobs):
    jobs = list(jobs)
    while jobs:
        jobs = step_all(jobs)


def side_by_side(jobs):
    jobs = list(jobs)
    while jobs:
        jobs = step_all(jobs)
        if jobs:
            yield


def each(count, step, body):
    def one(i, carry):
        body(pl.ds(pl.multiple_of(i * step, step), step))
        return carry

    lax.fori_loop(0, count // step, one, 0)


def aligned(start, size):
    return pl.ds(pl.multiple_of(start, size), size)


def add_rows(into, first, second):
    if isinstance(into, list):
        for refs in zip(into, first, second):
            add_rows(*refs)
        return
    lead, rows = into.shape[:-2], into.shape[-2]

    def add(spot):
        def body(window):
            spots = spot + (window,)
            into[spots] = first[spots] + second[spots]

        return body

    if not lead:
        each(rows, 16, add(()))
    else:
        for i in range(lead[0]):
            each(rows, 16, add((i,)))


def gather4(links, axis, own, block, arrived=None):
    me = links.here[axis]
    before, after, far = lax.rem(me + 3, 4), lax.rem(me + 1, 4), lax.rem(me + 2, 4)
    arrived = arrived or (lambda spot, side: None)
    up, down = {}, {}
    up[0] = links.send(own(0), block(me, 0), axis, 1)
    down[1] = links.send(own(1), block(me, 1), axis, 3)
    up[1] = links.send(own(1), block(me, 1), axis, 1)
    down[0] = links.send(own(0), block(me, 0), axis, 3)
    yield
    up[0].wait_recv()
    up_far = links.send(block(before, 0), block(before, 0), axis, 1)
    arrived(before, 0)
    down[1].wait_recv()
    down_far = links.send(block(after, 1), block(after, 1), axis, 3)
    arrived(after, 1)
    yield
    up[1].wait_recv()
    arrived(before, 1)
    down[0].wait_recv()
    arrived(after, 0)
    yield
    up_far.wait_recv()
    arrived(far, 0)
    down_far.wait_recv()
    arrived(far, 1)


def straight4(links, axis, own, block):
    me = links.here[axis]
    copies = [
        links.send(own(h), block(me, h), axis, step) for step in (2, 1, 3) for h in range(2)
    ]
    yield
    for copy in copies:
        copy.wait_recv()


def scatter4(links, axis, mine, near, far):
    me = links.here[axis]
    before, after, beyond = lax.rem(me + 3, 4), lax.rem(me + 1, 4), lax.rem(me + 2, 4)
    up_far = links.send(mine(beyond, 0), far[0], axis, 1)
    down_far = links.send(mine(beyond, 1), far[1], axis, 3)
    up_one = links.send(mine(after, 1), near[0](1), axis, 1)
    down_one = links.send(mine(before, 0), near[1](0), axis, 3)
    yield
    up_far.wait_recv()
    add_rows(far[0], far[0], mine(after, 0))
    up_two = links.send(far[0], near[0](0), axis, 1)
    down_far.wait_recv()
    add_rows(far[1], far[1], mine(before, 1))
    down_two = links.send(far[1], near[1](1), axis, 3)
    yield
    up_one.wait_recv()
    down_one.wait_recv()
    up_two.wait_recv()
    down_two.wait_recv()


def column_gather(links, own_ref, out):
    here = links.here
    rows = out.shape[1] // 2
    shared = []

    def own(h):
        return own_ref.at[pl.ds(h * rows, rows)]

    def block(p, h):
        return out.at[block_of(p, here["core"]), pl.ds(h * rows, rows)]

    def arrived(p, h):
        shared.append(links.send(block(p, h), block(p, h), "core"))

    ring = gather4(links, "y", own, block, arrived)
    next(ring)
    for h in range(2):
        shared.append(links.send(own(h), block(here["y"], h), "core"))
    yield
    for _ in ring:
        yield
    yield
    for copy in shared:
        copy.wait_recv()


def column_fetch(links, own, out, pieces):
    here = links.here
    y, core = here["y"], here["core"]
    y_lo = lax.rem(y, 2)
    rows = out.shape[1] // pieces
    spots = [pl.ds(q * rows, rows) for q in range(pieces)]
    spot, twin = block_of(y, core), block_of(y + 1 - 2 * y_lo, core)
    first, second = block_of(3 - y, core), block_of(2 - y + 2 * y_lo, core)
    across = [links.send(own(y_lo, w), out.at[spot, w], "cross") for w in spots]
    shared = [
        links.send(own(y_lo, pl.ds(0, out.shape[1])), out.at[spot], "core"),
        links.send(own(1 - y_lo, pl.ds(0, out.shape[1])), out.at[twin], "core"),
    ]
    passed = []
    for copy, w in zip(across, spots):
        yield
        copy.wait_recv()
        passed.append(links.send(out.at[first, w], out.at[first, w], "pair"))
        shared.append(links.send(out.at[first, w], out.at[first, w], "core"))
    for copy, w in zip(passed, spots):
        yield
        copy.wait_recv()
        shared.append(links.send(out.at[second, w], out.at[second, w], "core"))
    yield
    for copy in shared:
        copy.wait_recv()


class ColumnSum:
    def __init__(self, links, partial, passed, near, far, done):
        self.links, self.partial, self.done = links, partial, done
        self.passed, self.near, self.far = passed, near, far
        self.copies = {}

    def over(self, y_hi):
        core = self.links.here["core"]
        for y in (2 * y_hi, 2 * y_hi + 1):
            self.copies[y] = self.links.send(
                self.partial.at[block_of(y, 1 - core)], self.passed.at[y], "core"
            )

    def ring(self):
        links, partial, passed, near, far = (
            self.links,
            self.partial,
            self.passed,
            self.near,
            self.far,
        )
        core, me = links.here["core"], links.here["y"]
        before, after, beyond = lax.rem(me + 3, 4), lax.rem(me + 1, 4), lax.rem(me + 2, 4)
        rows = partial.shape[1] // 2

        def mine(p, h):
            return passed.at[p, pl.ds(h * rows, rows)]

        def add(p, h):
            add_rows(mine(p, h), mine(p, h), partial.at[block_of(p, core), pl.ds(h * rows, rows)])

        for y in range(4):
            self.copies[y].wait_recv()
        add(beyond, 0)
        up_far = links.send(mine(beyond, 0), far.at[0], "y", 1)
        add(beyond, 1)
        down_far = links.send(mine(beyond, 1), far.at[1], "y", 3)
        add(after, 1)
        up_one = links.send(mine(after, 1), near.at[0, pl.ds(rows, rows)], "y", 1)
        add(before, 0)
        down_one = links.send(mine(before, 0), near.at[1, pl.ds(0, rows)], "y", 3)
        add(after, 0)
        add(before, 1)
        yield
        up_far.wait_recv()
        add_rows(far.at[0], far.at[0], mine(after, 0))
        up_two = links.send(far.at[0], near.at[0, pl.ds(0, rows)], "y", 1)
        down_far.wait_recv()
        add_rows(far.at[1], far.at[1], mine(before, 1))
        down_two = links.send(far.at[1], near.at[1, pl.ds(rows, rows)], "y", 3)
        for h in range(2):
            add(me, h)
        yield
        up_one.wait_recv()
        down_one.wait_recv()
        up_two.wait_recv()
        down_two.wait_recv()
        total = passed.at[me]

        def body(window):
            self.done(
                window, full(total[window]) + (full(near[0, window]) + full(near[1, window]))
            )

        each(2 * rows, 16, body)


def column_scratch(rows):
    return [
        pltpu.VMEM((4, rows, 2048), LOW),
        pltpu.VMEM((2, rows, 2048), LOW),
        pltpu.VMEM((2, rows // 2, 2048), LOW),
    ]


class ByRows:
    def __init__(self, ref):
        self.ref = ref
        self.sides = [pl.ds(s * ref.shape[3] // 2, ref.shape[3] // 2) for s in range(2)]

    def own(self, own_ref, h, s):
        rows = own_ref.shape[0] // 2
        return [own_ref.at[pl.ds(h * rows, rows), self.sides[s]]]

    def one(self, z, x, h, s):
        rows = self.ref.shape[2] // 2
        return [self.ref.at[z, x, pl.ds(h * rows, rows), self.sides[s]]]

    def of_z(self, z, h, s):
        return [self.ref.at[z, pl.ds(2 * h, 2), :, self.sides[s]]]

    def of_x(self, x, h, s):
        return [self.ref.at[pl.ds(2 * h, 2), x, :, self.sides[s]]]


class ByColumns:
    def __init__(self, ref):
        self.ref = ref
        self.rows = ref.shape[0] // 2

    def own(self, own_ref, h, s):
        rows = self.rows // 2
        return [own_ref.at[pl.ds(s * self.rows + h * rows, rows)]]

    def one(self, z, x, h, s):
        rows = self.rows // 2
        return [self.ref.at[pl.ds(s * self.rows + h * rows, rows), aligned((z * 4 + x) * 128, 128)]]

    def of_z(self, z, h, s):
        return [self.ref.at[pl.ds(s * self.rows, self.rows), aligned(z * 512 + h * 256, 256)]]

    def of_x(self, x, h, s):
        return [
            self.ref.at[pl.ds(s * self.rows, self.rows), aligned((2 * h + k) * 512 + x * 128, 128)]
            for k in range(2)
        ]


def plane_first(links, blocks, own_ref, how):
    z, x = links.here["z"], links.here["x"]
    return side_by_side(
        [
            how(
                links,
                "x",
                lambda h: blocks.own(own_ref, h, 0),
                lambda p, h: blocks.one(z, p, h, 0),
            ),
            how(
                links,
                "z",
                lambda h: blocks.own(own_ref, h, 1),
                lambda p, h: blocks.one(p, x, h, 1),
            ),
        ]
    )


def plane_second(links, blocks, how):
    z, x = links.here["z"], links.here["x"]
    return side_by_side(
        [
            how(
                links, "z", lambda h: blocks.of_z(z, h, 0), lambda p, h: blocks.of_z(p, h, 0)
            ),
            how(
                links, "x", lambda h: blocks.of_x(x, h, 1), lambda p, h: blocks.of_x(p, h, 1)
            ),
        ]
    )


def plane_scratch(rows, width):
    return [
        pltpu.VMEM((2, 2, 4, rows, width), LOW),
        pltpu.VMEM((2, 2, 2, rows, width), LOW),
        pltpu.VMEM((2, 4, rows, width), LOW),
        pltpu.VMEM((2, 2, rows, width), LOW),
        pltpu.VMEM((2, 2, rows // 2, width), LOW),
    ]


def plane_scatter(links, grad, out, near, far, middle, near_two, far_two):
    z, x = links.here["z"], links.here["x"]
    by_rows = len(grad.shape) == 4
    rows, half = middle.shape[2:]

    def block(i, j, s):
        if by_rows:
            return grad.at[i, j, :, pl.ds(s * half, half)]
        return grad.at[pl.ds(s * rows, rows), aligned((i * 4 + j) * 128, 128)]

    def window_of(ref, s):
        if by_rows:
            return ref.at[:, pl.ds(s * half, half)]
        return ref.at[pl.ds(s * rows, rows)]

    def mine(s):
        if s == 0:
            return lambda p, h: [block(2 * h + k, p, 0) for k in range(2)]
        return lambda p, h: [block(p, 2 * h + k, 1) for k in range(2)]

    yield from side_by_side(
        [
            scatter4(
                links,
                axis,
                mine(s),
                [
                    lambda h, s=s, i=i: [near.at[s, i, 2 * h + k] for k in range(2)]
                    for i in range(2)
                ],
                [[far.at[s, i, k] for k in range(2)] for i in range(2)],
            )
            for s, axis in enumerate(("x", "z"))
        ]
    )
    for s in range(2):
        for p in range(4):
            own = block(p, x, 0) if s == 0 else block(z, p, 1)

            def body(window, s=s, p=p, own=own):
                middle[s, p, window] = low(
                    full(own[window])
                    + (full(near[s, 0, p, window]) + full(near[s, 1, p, window]))
                )

            each(rows, 16, body)
    part = rows // 2
    yield from side_by_side(
        [
            scatter4(
                links,
                axis,
                lambda p, h, s=s: middle.at[s, p, pl.ds(h * part, part)],
                [lambda h, s=s, i=i: near_two.at[s, i, pl.ds(h * part, part)] for i in range(2)],
                [far_two.at[s, 0], far_two.at[s, 1]],
            )
            for s, axis in enumerate(("z", "x"))
        ]
    )
    for s, me in enumerate((z, x)):
        into = window_of(out, s)

        def body(window, s=s, me=me, into=into):
            into[window] = low(
                full(middle[s, me, window])
                + (full(near_two[s, 0, window]) + full(near_two[s, 1, window]))
            )

        each(rows, 16, body)


def small_plane(links, own, out):
    z, x = links.here["z"], links.here["x"]
    out[z, x] = own[...]
    copies = [links.send(own, out.at[z, x], "x", step) for step in (1, 2, 3)]
    yield
    for copy in copies:
        copy.wait_recv()
    copies = [links.send(out.at[z], out.at[z], "z", step) for step in (1, 2, 3)]
    yield
    for copy in copies:
        copy.wait_recv()


def small_column(links, own, out):
    core, y = links.here["core"], links.here["y"]
    out[core, y] = own[...]
    copies = [links.send(own, out.at[core, y], "y", step) for step in (1, 2, 3)]
    yield
    for copy in copies:
        copy.wait_recv()
    copy = links.send(out.at[core], out.at[core], "core")
    yield
    copy.wait_recv()


def call(kernel, name, number, copies, kept, outs, out_specs, in_specs, scratch, vmem, operands):
    return pl.pallas_call(
        kernel,
        name=name,
        out_shape=outs,
        in_specs=in_specs,
        out_specs=out_specs,
        scratch_shapes=[
            pltpu.SemaphoreType.DMA((copies,)),
            pltpu.SemaphoreType.DMA((copies,)),
            pltpu.SemaphoreType.DMA((kept,)),
        ]
        + scratch,
        compiler_params=pltpu.CompilerParams(
            collective_id=number, has_side_effects=True, vmem_limit_bytes=vmem * 2**20
        ),
    )(*operands)


def shaped(shape, kind=LOW):
    return jax.ShapeDtypeStruct(shape, kind)


def turn_rows(values, cosine, sine):
    return values * cosine + pltpu.roll(values, HD // 2, 1) * sine


def forward_kernel(
    q_weight,
    k_weight,
    v_weight,
    o_weight,
    gate_weight,
    up_weight,
    down_weight,
    tokens,
    cotangent,
    gain_one,
    gain_two,
    gains,
    seq,
    waves,
    full_qkv_out,
    full_o_out,
    full_gu,
    full_d,
    unit_out,
    two_all,
    dy_all,
    middle,
    attended,
    queries,
    keys,
    values,
    proj,
    table,
    gains_all,
    starts,
    send_sems,
    recv_sems,
    kept,
    raw_qkv,
    own_qkv,
    own_o,
    raw_gu,
    own_gu,
    x_both,
    dy_both,
    down_own,
    full_qkv,
    full_o,
    unit_all,
    seq_all,
    partial,
    two_own,
    *column,
):
    links = Links(send_sems, recv_sems)
    local = Locals(kept)
    here = links.here
    z, x, y, core = here["z"], here["x"], here["y"], here["core"]
    half = lax.rem(y, 2)
    part = lax.div(y, 2) * 2 + core
    spot = block_of(y, core)
    plane = z * 4 + x
    own_rows = x_both.shape[0] // 2
    nq, nkv = own_o.shape[0], keys.shape[1]
    nff = raw_gu.shape[1] // 2

    load_x = local.start(tokens, x_both)
    load_qkv = [
        local.start(q_weight.at[:, aligned(part * nq, nq)], raw_qkv.at[:, pl.ds(0, nq)]),
        local.start(k_weight.at[:, aligned(part * nkv, nkv)], raw_qkv.at[:, pl.ds(nq, nkv)]),
        local.start(v_weight.at[:, aligned(part * nkv, nkv)], raw_qkv.at[:, pl.ds(nq + nkv, nkv)]),
    ]
    load_o = local.start(o_weight.at[aligned(part * nq, nq)], own_o)
    load_gu = [
        local.start(gate_weight.at[:, aligned(part * nff, nff)], raw_gu.at[:, pl.ds(0, nff)]),
        local.start(up_weight.at[:, aligned(part * nff, nff)], raw_gu.at[:, pl.ds(nff, nff)]),
    ]
    load_late = [
        local.start(down_weight.at[aligned(part * nff, nff)], down_own),
        local.start(cotangent, dy_both),
    ]
    links.meet(PLANE + COLUMN)
    load_x.wait()

    base = part * 2

    def norm_one(window):
        rows = pl.ds(pl.multiple_of(half * own_rows + window.start, 16), 16)
        value = full(x_both[rows])
        unit_all[spot, window] = low(value * inverse_of(value))

    each(own_rows, 16, norm_one)
    column_one = column_gather(links, unit_all.at[spot], unit_all)
    small = [small_column(links, seq, seq_all), small_plane(links, gains, gains_all)]
    step_all([column_one] + small)
    for copy in load_qkv:
        copy.wait()

    def scale_qkv(window):
        own_qkv[window] = low(full(raw_qkv[window]) * gain_one[window])
        full_qkv[z, x, window] = own_qkv[window]

    each(own_rows, 16, scale_qkv)
    blocks_qkv, blocks_o = ByRows(full_qkv), ByColumns(full_o)
    blocks_gu, blocks_d = ByRows(full_gu), ByColumns(full_d)
    first_qkv = plane_first(links, blocks_qkv, own_qkv, straight4)
    step_all([first_qkv])
    load_o.wait()
    first_o = plane_first(links, blocks_o, own_o, straight4)
    keep_o = local.start(own_o, full_o.at[:, aligned(plane * 128, 128)])
    for copy in load_gu + load_late:
        copy.wait()

    def scale_gu(window):
        own_gu[window] = low(full(raw_gu[window]) * gain_two[window])

    each(own_rows, 16, scale_gu)
    step_all([first_o])
    first_late = [
        plane_first(links, blocks_gu, own_gu, straight4),
        plane_first(links, blocks_d, down_own, straight4),
    ]
    step_all(first_late)
    keep_gu = local.start(own_gu, full_gu.at[z, x])
    keep_d = local.start(down_own, full_d.at[:, aligned(plane * 128, 128)])
    late = [
        local.start(dy_both.at[pl.ds(i * own_rows, own_rows)], dy_all.at[base + i])
        for i in range(2)
    ]
    together([first_qkv])
    second_qkv = plane_second(links, blocks_qkv, gather4)
    step_all([second_qkv, column_one] + small)
    together(small)

    ids = full(seq_all[...])
    count_0 = jnp.sum((ids < 0.5).astype(WIDE), (0, 1))
    count_01 = jnp.sum((ids < 1.5).astype(WIDE), (0, 1))
    start_1 = jnp.sum(count_0[0:1], 1, keepdims=True)
    start_2 = jnp.sum(count_01[0:1], 1, keepdims=True)
    starts[0:4] = jnp.broadcast_to(start_1, (4, HD))
    starts[4:8] = jnp.broadcast_to(start_2, (4, HD))

    def start_of(index):
        return jnp.where(index < start_1, 0.0, jnp.where(index < start_2, start_1, start_2))

    def tables(i, carry):
        window = aligned(i * 64, 64)
        index = full(lax.broadcasted_iota(jnp.int32, (64, HD), 0) + i * 64)
        angle = (index - start_of(index)) * waves[0:1]
        table[0, window] = jnp.cos(angle)
        table[1, window] = jnp.sin(angle) * waves[1:2]
        return carry

    lax.fori_loop(0, 6, tables, 0)
    step_all([column_one, second_qkv])
    together([first_o])
    keep_o.wait()
    second_o = plane_second(links, blocks_o, gather4)
    step_all([second_o])
    lax.fori_loop(6, 12, tables, 0)
    step_all([column_one, second_qkv])
    lax.fori_loop(12, 16, tables, 0)
    together([second_qkv, column_one])
    step_all([second_o])
    together(first_late)
    keep_gu.wait()
    keep_d.wait()
    second_late = [
        plane_second(links, blocks_gu, gather4),
        plane_second(links, blocks_d, gather4),
    ]
    step_all(second_late)
    column_dy = column_fetch(
        links,
        lambda i, w: dy_both.at[
            pl.ds(pl.multiple_of(i * own_rows + w.start, w.size), w.size)
        ],
        dy_all,
        4,
    )
    step_all([column_dy])
    late += [
        local.start(full_qkv, full_qkv_out),
        local.start(unit_all, unit_out),
    ]

    gain_rows = jnp.sum(gains_all[...], (0, 1))
    q_gain, k_gain = gain_rows[0:1], gain_rows[1:2]

    def project(i, carry):
        window = aligned(i * 256, 256)
        unit = unit_all[pl.ds(2 * i, 2)].reshape(256, unit_all.shape[2])
        weights = full_qkv[...].reshape(16 * own_rows, nq + 2 * nkv)
        out = dot_nn(unit, weights)
        cosine, sine = table[0, window], table[1, window]
        for head in range(3):
            value = out[:, head * HD : (head + 1) * HD]
            proj[head, window] = value
            gain = q_gain if head < 2 else k_gain
            rotated = low(turn_rows(value * inverse_of(value) * gain, cosine, sine))
            if head < 2:
                queries[head, window] = rotated
            else:
                keys[window] = rotated
        values[window] = low(out[:, 3 * HD :])
        return carry

    lax.fori_loop(0, 4, project, 0)
    together([second_o])
    late.append(local.start(full_o, full_o_out))
    step_all([column_dy])

    def turn_done(window, total):
        rows = pl.ds(pl.multiple_of(half * own_rows + window.start, 16), 16)
        value = full(x_both[rows]) + total
        middle[window] = value
        two_own[window] = low(value * inverse_of(value))

    summed = ColumnSum(links, partial, *column, turn_done)
    for i in range(4):
        window = pl.ds(i * 256, 256)
        seen = 256 * (i + 1)
        query = jnp.concatenate([queries[0, window], queries[1, window]], 0)
        scores = dot_nt(query, keys[0:seen]) * SCALE
        row = lax.broadcasted_iota(jnp.int32, (256, 1), 0) + i * 256
        row = full(jnp.concatenate([row, row], 0))
        column_index = full(lax.broadcasted_iota(jnp.int32, (512, seen), 1))
        seen_here = (column_index <= row) & (column_index >= start_of(row))
        scores = jnp.where(seen_here, scores, -jnp.inf)
        power = jnp.exp(scores - jnp.max(scores, -1, keepdims=True))
        probs = power * (1.0 / jnp.sum(power, -1, keepdims=True))
        mixed = low(dot_nn(low(probs), values[0:seen]))
        both = jnp.concatenate([mixed[:256], mixed[256:]], 1)
        attended[window] = both
        partial[2 * i : 2 * i + 2] = low(dot_nn(both, full_o[...])).reshape(
            2, own_rows, partial.shape[2]
        )
        if i % 2:
            summed.over(i // 2)
        if i > 0:
            step_all([column_dy])
    ring = summed.ring()
    step_all([ring])
    step_all([ring])
    step_all(second_late)
    together([ring])
    late.append(local.start(two_own, two_all.at[spot]))
    column_two = column_gather(links, two_own, two_all)
    step_all([column_two])
    step_all([column_two])
    together([column_two, column_dy])
    together(second_late)
    for copy in late:
        copy.wait()
    links.drain()


def middle_kernel(
    full_gu,
    full_d,
    two_all,
    dy_all,
    middle,
    mid_all,
    grad_gu_w,
    grad_mid,
    result,
    sum_d,
    down_part,
    send_sems,
    recv_sems,
    kept,
    gu,
    down,
    two,
    dy,
    product,
    grad_gu,
    partial,
    partial_down,
    grad_d,
    dy_own,
    mid_own,
    *scratch,
):
    column, column_down = scratch[:3], scratch[3:6]
    plane_d = scratch[6:]
    links = Links(send_sems, recv_sems)
    local = Locals(kept)
    here = links.here
    spot = block_of(here["y"], here["core"])
    rows = partial.shape[1] // 2
    width = partial.shape[2]
    nff = product.shape[1]
    windows = [pl.ds(h * rows, rows) for h in range(2)]
    halves = [pl.ds(h * 8 * rows, 8 * rows) for h in range(2)]

    load_gu = local.start(full_gu, gu)
    load_two = [local.start(two_all.at[:, windows[h]], two.at[h]) for h in range(2)]
    load_d = local.start(full_d, down)
    load_dy = [local.start(dy_all.at[:, windows[h]], dy.at[h]) for h in range(2)]
    load_own = local.start(dy_all.at[spot], dy_own)
    links.meet([("x", 1), ("x", 3), ("z", 1), ("z", 3), ("y", 1), ("y", 3), ("core", 0)])

    def loop(first, last, body):
        def one(i, carry):
            body(i)
            return carry

        lax.fori_loop(first, last, one, 0)

    def units(h, first, last):
        def body(j):
            at, after = aligned(j * 256, 256), aligned(nff + j * 256, 256)
            unit = two[h].reshape(8 * rows, width)
            gate = dot_nn(unit, gu[:, :, :, at].reshape(width, 256))
            up = dot_nn(unit, gu[:, :, :, after].reshape(width, 256))
            grad = dot_nt(dy[h].reshape(8 * rows, width), down[at])
            sigmoid = 1.0 / (1.0 + jnp.exp(-gate))
            silu = gate * sigmoid
            product[halves[h], at] = low(silu * up)
            grad_gu[halves[h], at] = low(grad * up * (sigmoid * (1.0 + gate * (1.0 - sigmoid))))
            grad_gu[halves[h], after] = low(grad * silu)

        loop(first, last, body)

    def forward_part(h):
        def body(n):
            at = aligned(n * 512, 512)
            out = low(dot_nn(product[halves[h]], down[:, at]))
            partial_down[:, windows[h], at] = out.reshape(8, rows, 512)

        loop(0, width // 512, body)

    def backward_part(h, first, last):
        def body(n):
            out = low(dot_nt(grad_gu[halves[h]], gu[n].reshape(512, 2 * nff)))
            partial[:, windows[h], aligned(n * 512, 512)] = out.reshape(8, rows, 512)

        loop(first, last, body)

    def here_rows(h, window):
        return pl.ds(pl.multiple_of(h * rows + window.start, 16), 16)

    def done(h):
        def body(window, total):
            at = here_rows(h, window)
            value = middle[at]
            inverse = inverse_of(value)
            value = full(dy_own[at]) + norm_back(total, value * inverse, inverse)
            grad_mid[at] = value
            mid_own[at] = low(value)

        return body

    def done_down(h):
        def body(window, total):
            at = here_rows(h, window)
            result[at] = low(middle[at] + total)

        return body

    def column_sum(source, parts, h, body):
        passed, near, far = parts
        return ColumnSum(
            links,
            source.at[:, windows[h]],
            passed.at[:, windows[h]],
            near.at[:, windows[h]],
            far.at[:, pl.ds(h * rows // 2, rows // 2)],
            body(h),
        )

    sums = [column_sum(partial, column, h, done) for h in range(2)]
    sum_down = column_sum(partial_down, column_down, 0, done_down)
    rings = [one.ring() for one in sums]
    ring_down = sum_down.ring()
    gathers = [
        column_gather(links, mid_own.at[windows[h]], mid_all.at[:, windows[h]]) for h in range(2)
    ]
    load_gu.wait()
    load_two[0].wait()
    load_d.wait()
    load_dy[0].wait()
    load_own.wait()
    def down_grad(i):
        at = aligned(i * 256, 256)
        grad_d[at] = low(dot_tn(product[:, at], dy[...].reshape(16 * rows, width)))

    def gate_up_grad(i):
        acts = two[:, :, :, aligned(i * 512, 512)].reshape(16 * rows, 512)
        gu[i] = low(dot_tn(acts, grad_gu[...])).reshape(4, 128, 2 * nff)

    units(0, 0, nff // 256)
    forward_part(0)
    sum_down.over(0)
    sum_down.over(1)
    backward_part(0, 0, 2)
    step_all([ring_down])
    backward_part(0, 2, 4)
    sums[0].over(0)
    sums[0].over(1)
    load_two[1].wait()
    load_dy[1].wait()
    units(1, 0, 1)
    step_all([rings[0]])
    units(1, 1, nff // 256)
    step_all([ring_down, rings[0]])
    loop(0, nff // 256, down_grad)
    scatter_d = plane_scatter(links, grad_d, sum_d, *plane_d)
    step_all([scatter_d])
    together([rings[0]])
    step_all([gathers[0]])
    step_all([gathers[0]])
    backward_part(1, 0, 4)
    sums[1].over(0)
    sums[1].over(1)
    together([ring_down])
    loop(0, 2, gate_up_grad)
    step_all([rings[1], gathers[0]])
    loop(2, 4, gate_up_grad)
    keep_w = local.start(gu, grad_gu_w)
    step_all([scatter_d, rings[1], gathers[0]])
    forward_part(1)
    keep_down = local.start(partial_down.at[:, windows[1]], down_part)
    step_all([scatter_d])
    together([rings[1]])
    step_all([gathers[1]])
    step_all([gathers[1]])
    step_all([scatter_d])
    keep_mid = local.start(mid_own, mid_all.at[spot])
    step_all([gathers[1], gathers[0], scatter_d])
    together([gathers[1], gathers[0], scatter_d])
    for copy in (keep_w, keep_mid, keep_down):
        copy.wait()
    links.drain()


def end_kernel(
    q_weight,
    k_weight,
    v_weight,
    gate_weight,
    up_weight,
    tokens,
    full_qkv,
    full_o,
    unit_all,
    mid_all,
    grad_gu_w,
    attended,
    queries,
    keys,
    values,
    proj,
    table,
    gains_all,
    starts,
    gain_one,
    gain_two,
    grad_mid,
    middle,
    result,
    sum_d,
    down_part,
    grad_x,
    out_rows,
    all_qkv,
    all_o,
    all_gu,
    all_d,
    sums_out,
    send_sems,
    recv_sems,
    kept,
    weights,
    weight_o,
    unit,
    mid,
    grad_gu,
    grad_o,
    grad_qkv_w,
    raw_qkv,
    raw_gu,
    x_own,
    grad_att,
    dk,
    dv,
    grad_qkv,
    sum_gu,
    sum_qkv,
    own_o,
    own_gu,
    own_qkv,
    small,
    small_all,
    row,
    row_all,
    turned,
    x_pair,
    row_pair,
    part_down,
    *scratch,
):
    column_parts, column_down = scratch[:3], scratch[3:6]
    plane_gu, plane_o, plane_qkv = scratch[6:11], scratch[11:16], scratch[16:]
    links = Links(send_sems, recv_sems)
    local = Locals(kept)
    here = links.here
    y, core = here["y"], here["core"]
    half = lax.rem(y, 2)
    part = lax.div(y, 2) * 2 + core
    part_other = lax.div(lax.rem(y + 2, 4), 2) * 2 + core
    rows, width = x_own.shape
    nq, nkv = own_o.shape[0], keys.shape[1]
    nff = sum_gu.shape[1] // 2

    load_mid = local.start(mid_all, mid)
    load_o = local.start(full_o, weight_o)
    load_gu = local.start(grad_gu_w, grad_gu)
    load_down = local.start(down_part, part_down)
    loads = [
        local.start(full_qkv, weights),
        local.start(unit_all, unit),
        local.start(tokens.at[aligned(half * rows, rows)], x_own),
        local.start(q_weight.at[:, aligned(part * nq, nq)], raw_qkv.at[:, pl.ds(0, nq)]),
        local.start(k_weight.at[:, aligned(part * nkv, nkv)], raw_qkv.at[:, pl.ds(nq, nkv)]),
        local.start(v_weight.at[:, aligned(part * nkv, nkv)], raw_qkv.at[:, pl.ds(nq + nkv, nkv)]),
        local.start(gate_weight.at[:, aligned(part * nff, nff)], raw_gu.at[:, pl.ds(0, nff)]),
        local.start(up_weight.at[:, aligned(part * nff, nff)], raw_gu.at[:, pl.ds(nff, nff)]),
    ]
    links.meet(PLANE + COLUMN)

    def share(own, out):
        across = links.send(own, out.at[part], "y", 2)
        beside = links.send(own, out.at[part], "core")
        keep = local.start(own, out.at[part])
        yield
        across.wait_recv()
        second = links.send(out.at[part_other], out.at[part_other], "core")
        yield
        beside.wait_recv()
        second.wait_recv()
        keep.wait()

    def exchange(own, out):
        copy = links.send(own, out.at[half], "pair")
        keep = local.start(own, out.at[half])
        yield
        copy.wait_recv()
        keep.wait()

    def done_down(window, total):
        late = pl.ds(pl.multiple_of(rows // 2 + window.start, 16), 16)
        row_pair[window] = result[window]
        row_pair[late] = low(middle[late] + total)

    def done_one(window, total):
        value = full(x_own[window])
        inverse = inverse_of(value)
        x_pair[window] = low(grad_mid[window] + norm_back(total, value * inverse, inverse))

    def scale(into, total, raw, gain, spot):
        def body(window):
            into[window] = low(full(total[window]) * gain[window])
            part_sum = jnp.sum(full(total[window]) * full(raw[window]), 1, keepdims=True)
            turned[spot, window] = jnp.broadcast_to(part_sum, (16, HD))

        each(rows, 16, body)

    load_mid.wait()
    load_o.wait()

    def attended_grad(i, carry):
        window = aligned(i * 256, 256)
        out = low(dot_nt(mid[pl.ds(2 * i, 2)].reshape(256, width), weight_o[...]))
        grad_att[0, window] = out[:, :HD]
        grad_att[1, window] = out[:, HD:]
        return carry

    def gu_job():
        yield from plane_scatter(links, grad_gu, sum_gu, *plane_gu)
        scale(own_gu, sum_gu, raw_gu, gain_two, 1)
        yield from share(own_gu, all_gu)

    def o_job():
        yield from plane_scatter(links, grad_o, own_o, *plane_o)
        yield from share(own_o, all_o)

    def qkv_job():
        yield from plane_scatter(links, grad_qkv_w, sum_qkv, *plane_qkv)
        scale(own_qkv, sum_qkv, raw_qkv, gain_one, 0)
        yield from share(own_qkv, all_qkv)

    job_gu, job_o, job_qkv = gu_job(), o_job(), qkv_job()
    sum_down = ColumnSum(links, part_down, *column_down, done_down)
    ring_down = sum_down.ring()
    share_d = share(sum_d, all_d)
    load_gu.wait()
    step_all([job_gu])
    load_down.wait()
    sum_down.over(0)
    sum_down.over(1)
    lax.fori_loop(0, 4, attended_grad, 0)

    gain_rows = jnp.sum(gains_all[...], (0, 1))
    q_gain, k_gain = gain_rows[0:1], gain_rows[1:2]
    start_1, start_2 = starts[0:1, 0:1], starts[4:5, 0:1]
    dk[...] = jnp.zeros_like(dk)
    dv[...] = jnp.zeros_like(dv)
    small[...] = jnp.zeros_like(small)

    def project_back(grad, head, window, gain):
        cosine, sine = table[0, window], table[1, window]
        back = grad * cosine - pltpu.roll(grad, HD // 2, 1) * sine
        value = proj[head, window]
        inverse = inverse_of(value)
        scaled = value * inverse
        spot = 0 if head < 2 else 1
        small[spot : spot + 1] += jnp.sum(back * scaled, 0, keepdims=True)
        return low(norm_back(back * gain, scaled, inverse))

    for i in range(4):
        window = pl.ds(i * 256, 256)
        seen = 256 * (i + 1)
        query = jnp.concatenate([queries[0, window], queries[1, window]], 0)
        grad = jnp.concatenate([grad_att[0, window], grad_att[1, window]], 0)
        key, value = keys[0:seen], values[0:seen]
        scores = dot_nt(key, query) * SCALE
        column = lax.broadcasted_iota(jnp.int32, (1, 256), 1) + i * 256
        column = full(jnp.concatenate([column, column], 1))
        start = jnp.where(
            column < start_1, 0.0, jnp.where(column < start_2, start_1, start_2)
        )
        index = full(lax.broadcasted_iota(jnp.int32, (seen, 512), 0))
        scores = jnp.where((index <= column) & (index >= start), scores, -jnp.inf)
        power = jnp.exp(scores - jnp.max(scores, 0, keepdims=True))
        probs = power * (1.0 / jnp.sum(power, 0, keepdims=True))
        grad_probs = dot_nt(value, grad)
        inner = jnp.sum(probs * grad_probs, 0, keepdims=True)
        grad_scores = low(probs * (grad_probs - inner))
        dv[0:seen] += dot_nn(low(probs), grad)
        dk[0:seen] += dot_nn(grad_scores, query)
        dq = dot_tn(key, grad_scores).T * SCALE
        for head in range(2):
            grad_qkv[window, head * HD : (head + 1) * HD] = project_back(
                dq[head * 256 : (head + 1) * 256], head, window, q_gain
            )
        if i == 0:
            step_all([ring_down])
        if i == 2:
            step_all([ring_down, share_d])

    def keys_back(i, carry):
        window = aligned(i * 256, 256)
        grad_qkv[window, nq : nq + nkv] = project_back(dk[window] * SCALE, 2, window, k_gain)
        grad_qkv[window, nq + nkv :] = low(dv[window])
        return carry

    lax.fori_loop(0, 4, keys_back, 0)
    small_job = small_plane(links, small, small_all)
    step_all([small_job])

    def unit_grad(i, carry):
        out = low(
            dot_nt(
                grad_qkv[aligned(i * 256, 256)], weights[...].reshape(width, nq + 2 * nkv)
            )
        )
        mid[pl.ds(2 * i, 2)] = out.reshape(2, rows, width)
        return carry

    for copy in loads:
        copy.wait()
    sum_one = ColumnSum(links, mid, *column_parts, done_one)
    grad_o[...] = low(dot_tn(attended[...], mid[...].reshape(8 * rows, width)))
    step_all([job_o])
    together([ring_down])
    pair_rows = exchange(row_pair, out_rows)
    step_all([pair_rows])
    lax.fori_loop(0, 2, unit_grad, 0)
    sum_one.over(0)
    lax.fori_loop(2, 4, unit_grad, 0)
    sum_one.over(1)
    step_all([job_gu])
    ring_one = sum_one.ring()
    step_all([ring_one])

    def weight_grad(i, carry):
        at = aligned(i * 512, 512)
        out = dot_tn(unit[:, :, at].reshape(8 * rows, 512), grad_qkv[...])
        grad_qkv_w[i] = low(out).reshape(4, rows, nq + 2 * nkv)
        return carry

    lax.fori_loop(0, 4, weight_grad, 0)
    step_all([job_qkv, job_gu, job_o, small_job])
    step_all([share_d, job_o])
    step_all([ring_one])
    step_all([job_gu, job_qkv, job_o])
    step_all([job_gu, job_qkv, small_job])
    together([ring_one])
    pair_x = exchange(x_pair, grad_x)
    step_all([pair_x, job_gu, job_qkv])
    step_all([job_gu, job_qkv])
    row[0:2] = jnp.sum(small_all[:, :, 0:2], (0, 1))
    row[2:3] = turned[0].T[0:1]
    row[3:4] = turned[1].T[0:1]
    row[4:8] = jnp.zeros((4, HD), WIDE)
    row_job = small_column(links, row, row_all)
    step_all([row_job, job_o, job_gu, job_qkv])
    together([job_o, job_gu, job_qkv, row_job, share_d, pair_rows])
    together([pair_x])
    sums_out[...] = jnp.sum(row_all[...], (0, 1))
    links.drain()


def widen_kernel(
    out_rows,
    grad_x,
    all_qkv,
    all_o,
    all_gu,
    all_d,
    out_final,
    x_final,
    q_final,
    k_final,
    v_final,
    o_final,
    gate_final,
    up_final,
    d_final,
    rows_low,
    x_low,
    qkv_low,
    o_low,
    gu_low,
    d_low,
    x_wide,
    q_wide,
    k_wide,
    v_wide,
    o_wide,
    gate_wide,
    up_wide,
    d_wide,
    kept,
):
    local = Locals(kept)
    halves, rows, _ = x_low.shape
    parts, rows_w = gu_low.shape[:2]
    nff = gu_low.shape[2] // 2
    load_gu = local.start(all_gu, gu_low)
    load_d = local.start(all_d, d_low)
    load_qkv = local.start(all_qkv, qkv_low)
    load_o = local.start(all_o, o_low)
    load_x = local.start(grad_x, x_low)
    load_rows = local.start(out_rows, rows_low)
    nq = q_wide.shape[1] // parts
    nkv = k_wide.shape[1] // parts
    stores = []

    def side_by_side_parts(source, start, size, into, final):
        for c in range(parts):

            def body(window, c=c):
                into[window, c * size : (c + 1) * size] = full(
                    source[c, window, start : start + size]
                )

            each(rows_w, 32, body)
        stores.append(local.start(into, final))

    def stacked(source, into, final, step):
        count, size = source.shape[:2]
        for c in range(count):

            def body(window, c=c):
                into[c, window] = full(source[c, window])

            each(size, step, body)
            stores.append(local.start(into.at[c], final.at[pl.ds(c * size, size)]))

    load_gu.wait()
    side_by_side_parts(gu_low, 0, nff, gate_wide, gate_final)
    side_by_side_parts(gu_low, nff, nff, up_wide, up_final)
    load_d.wait()
    stacked(d_low, d_wide, d_final, 128)
    load_x.wait()
    stacked(x_low, x_wide, x_final, 16)
    load_rows.wait()
    for c in range(halves):
        stores.append(local.start(rows_low.at[c], out_final.at[pl.ds(c * rows, rows)]))
    load_qkv.wait()
    side_by_side_parts(qkv_low, 0, nq, q_wide, q_final)
    side_by_side_parts(qkv_low, nq, nkv, k_wide, k_final)
    side_by_side_parts(qkv_low, nq + nkv, nkv, v_wide, v_final)
    load_o.wait()
    stacked(o_low, o_wide, o_final, 128)
    for copy in stores:
        copy.wait()


def per_device(
    tokens,
    segments,
    attn_gain,
    q_weight,
    k_weight,
    v_weight,
    q_gain,
    k_gain,
    o_weight,
    mlp_gain,
    gate_weight,
    up_weight,
    down_weight,
    cotangent,
):
    parts, halves = lax.axis_size("ctx"), lax.axis_size("tp")
    half = lax.axis_index("tp")
    rows_here, width = tokens.shape
    seq_len = rows_here * parts
    own_rows = rows_here // halves
    blocks = parts * halves

    def own(array):
        return lax.dynamic_slice_in_dim(array, half * own_rows, own_rows, 0)

    attn_gain_f = jnp.broadcast_to(full(attn_gain)[:, None], (attn_gain.shape[0], 1))
    mlp_gain_f = jnp.broadcast_to(full(mlp_gain)[:, None], (mlp_gain.shape[0], 1))
    rows_w = q_weight.shape[0]
    nq, nkv, nff = q_weight.shape[1] // parts, k_weight.shape[1] // parts, gate_weight.shape[1] // parts
    na, nb = nq + 2 * nkv, 2 * nff
    few = q_gain.shape[0]
    gains = lax.dynamic_update_slice(
        jnp.zeros((8, HD), WIDE),
        full(jnp.stack([q_gain, k_gain])),
        (0, lax.axis_index("fsdp") * few),
    )
    seq = jnp.broadcast_to(own(segments)[None, :], (8, own_rows))
    frequency = jnp.power(rope_base, -2.0 * jnp.arange(HD // 2, dtype=WIDE) / HD)
    ones = jnp.ones((HD // 2,), WIDE)
    waves = jnp.zeros((8, HD), WIDE).at[0].set(jnp.tile(frequency, 2))
    waves = waves.at[1].set(jnp.concatenate([-ones, ones]))

    (
        full_qkv,
        full_o,
        full_gu,
        full_d,
        unit_all,
        two_all,
        dy_all,
        middle,
        attended,
        queries,
        keys,
        values,
        proj,
        table,
        gains_all,
        starts,
    ) = call(
        forward_kernel,
        "forward",
        0,
        176,
        24,
        (
            shaped((4, 4, rows_w, na)),
            shaped((nq, width)),
            shaped((4, 4, rows_w, nb)),
            shaped((nff, width)),
            shaped((blocks, own_rows, width)),
            shaped((blocks, own_rows, width)),
            shaped((blocks, own_rows, width)),
            shaped((own_rows, width), WIDE),
            shaped((seq_len, nq)),
            shaped((2, seq_len, HD)),
            shaped((seq_len, HD)),
            shaped((seq_len, HD)),
            shaped((3, seq_len, HD), WIDE),
            shaped((2, seq_len, HD), WIDE),
            shaped((4, 4, 8, HD), WIDE),
            shaped((8, HD), WIDE),
        ),
        [HBM] * 7 + [VMEM] * 9,
        [HBM] * 9 + [VMEM] * 5,
        [
            pltpu.VMEM((rows_w, na), LOW),
            pltpu.VMEM((rows_w, na), LOW),
            pltpu.VMEM((nq, rows_w), LOW),
            pltpu.VMEM((rows_w, nb), LOW),
            pltpu.VMEM((rows_w, nb), LOW),
            pltpu.VMEM((rows_here, width), LOW),
            pltpu.VMEM((rows_here, width), LOW),
            pltpu.VMEM((nff, rows_w), LOW),
            pltpu.VMEM((4, 4, rows_w, na), LOW),
            pltpu.VMEM((nq, width), LOW),
            pltpu.VMEM((blocks, own_rows, width), LOW),
            pltpu.VMEM((2, 4, 8, own_rows), jnp.int32),
            pltpu.VMEM((blocks, own_rows, width), LOW),
            pltpu.VMEM((own_rows, width), LOW),
        ]
        + column_scratch(own_rows),
        58,
        (
            q_weight,
            k_weight,
            v_weight,
            o_weight,
            gate_weight,
            up_weight,
            down_weight,
            tokens,
            cotangent,
            attn_gain_f,
            mlp_gain_f,
            gains,
            seq,
            waves,
        ),
    )

    mid_all, grad_gu_w, grad_mid, result, sum_d, down_part = call(
        middle_kernel,
        "middle",
        1,
        144,
        12,
        (
            shaped((blocks, own_rows, width)),
            shaped((4, 4, rows_w, nb)),
            shaped((own_rows, width), WIDE),
            shaped((own_rows, width)),
            shaped((nff, rows_w)),
            shaped((blocks, own_rows // 2, width)),
        ),
        [HBM] * 2 + [VMEM] * 3 + [HBM],
        [HBM] * 4 + [VMEM],
        [
            pltpu.VMEM((4, 4, rows_w, nb), LOW),
            pltpu.VMEM((nff, width), LOW),
            pltpu.VMEM((2, blocks, own_rows // 2, width), LOW),
            pltpu.VMEM((2, blocks, own_rows // 2, width), LOW),
            pltpu.VMEM((seq_len, nff), LOW),
            pltpu.VMEM((seq_len, nb), LOW),
            pltpu.VMEM((blocks, own_rows, width), LOW),
            pltpu.VMEM((blocks, own_rows, width), LOW),
            pltpu.VMEM((nff, width), LOW),
            pltpu.VMEM((own_rows, width), LOW),
            pltpu.VMEM((own_rows, width), LOW),
        ]
        + column_scratch(own_rows)
        + column_scratch(own_rows // 2)
        + plane_scratch(nff // 2, rows_w),
        62,
        (full_gu, full_d, two_all, dy_all, middle),
    )

    grad_x, out_rows, all_qkv, all_o, all_gu, all_d, sums = call(
        end_kernel,
        "end",
        2,
        160,
        40,
        (
            shaped((halves, own_rows, width)),
            shaped((halves, own_rows, width)),
            shaped((parts, rows_w, na)),
            shaped((parts, nq, rows_w)),
            shaped((parts, rows_w, nb)),
            shaped((parts, nff, rows_w)),
            shaped((8, HD), WIDE),
        ),
        [HBM] * 6 + [VMEM],
        [HBM] * 11 + [VMEM] * 14 + [HBM],
        [
            pltpu.VMEM((4, 4, rows_w, na), LOW),
            pltpu.VMEM((nq, width), LOW),
            pltpu.VMEM((blocks, own_rows, width), LOW),
            pltpu.VMEM((blocks, own_rows, width), LOW),
            pltpu.VMEM((4, 4, rows_w, nb), LOW),
            pltpu.VMEM((nq, width), LOW),
            pltpu.VMEM((4, 4, rows_w, na), LOW),
            pltpu.VMEM((rows_w, na), LOW),
            pltpu.VMEM((rows_w, nb), LOW),
            pltpu.VMEM((own_rows, width), LOW),
            pltpu.VMEM((2, seq_len, HD), LOW),
            pltpu.VMEM((seq_len, HD), WIDE),
            pltpu.VMEM((seq_len, HD), WIDE),
            pltpu.VMEM((seq_len, na), LOW),
            pltpu.VMEM((rows_w, nb), LOW),
            pltpu.VMEM((rows_w, na), LOW),
            pltpu.VMEM((nq, rows_w), LOW),
            pltpu.VMEM((rows_w, nb), LOW),
            pltpu.VMEM((rows_w, na), LOW),
            pltpu.VMEM((8, HD), WIDE),
            pltpu.VMEM((4, 4, 8, HD), WIDE),
            pltpu.VMEM((8, HD), WIDE),
            pltpu.VMEM((2, 4, 8, HD), WIDE),
            pltpu.VMEM((2, rows_w, HD), WIDE),
            pltpu.VMEM((own_rows, width), LOW),
            pltpu.VMEM((own_rows, width), LOW),
            pltpu.VMEM((blocks, own_rows // 2, width), LOW),
        ]
        + column_scratch(own_rows)
        + column_scratch(own_rows // 2)
        + plane_scratch(rows_w, nb // 2)
        + plane_scratch(nq // 2, rows_w)
        + plane_scratch(rows_w, na // 2),
        62,
        (
            q_weight,
            k_weight,
            v_weight,
            gate_weight,
            up_weight,
            tokens,
            full_qkv,
            full_o,
            unit_all,
            mid_all,
            grad_gu_w,
            attended,
            queries,
            keys,
            values,
            proj,
            table,
            gains_all,
            starts,
            attn_gain_f,
            mlp_gain_f,
            grad_mid,
            middle,
            result,
            sum_d,
            down_part,
        ),
    )

    (
        out_final,
        x_final,
        q_final,
        k_final,
        v_final,
        o_final,
        gate_final,
        up_final,
        d_final,
    ) = pl.pallas_call(
        widen_kernel,
        name="widen",
        out_shape=(
            shaped((rows_here, width)),
            shaped((rows_here, width), WIDE),
            shaped(q_weight.shape, WIDE),
            shaped(k_weight.shape, WIDE),
            shaped(v_weight.shape, WIDE),
            shaped(o_weight.shape, WIDE),
            shaped(gate_weight.shape, WIDE),
            shaped(up_weight.shape, WIDE),
            shaped(down_weight.shape, WIDE),
        ),
        in_specs=[HBM] * 6,
        out_specs=[HBM] * 9,
        scratch_shapes=[
            pltpu.VMEM((halves, own_rows, width), LOW),
            pltpu.VMEM((halves, own_rows, width), LOW),
            pltpu.VMEM((parts, rows_w, na), LOW),
            pltpu.VMEM((parts, nq, rows_w), LOW),
            pltpu.VMEM((parts, rows_w, nb), LOW),
            pltpu.VMEM((parts, nff, rows_w), LOW),
            pltpu.VMEM((halves, own_rows, width), WIDE),
            pltpu.VMEM(q_weight.shape, WIDE),
            pltpu.VMEM(k_weight.shape, WIDE),
            pltpu.VMEM(v_weight.shape, WIDE),
            pltpu.VMEM((parts, nq, rows_w), WIDE),
            pltpu.VMEM(gate_weight.shape, WIDE),
            pltpu.VMEM(up_weight.shape, WIDE),
            pltpu.VMEM((parts, nff, rows_w), WIDE),
            pltpu.SemaphoreType.DMA((40,)),
        ],
        compiler_params=pltpu.CompilerParams(vmem_limit_bytes=60 * 2**20),
    )(out_rows, grad_x, all_qkv, all_o, all_gu, all_d)
    sum_qk = lax.dynamic_slice_in_dim(sums[:2], lax.axis_index("fsdp") * few, few, 1)
    return (
        out_final,
        x_final,
        sums[2],
        q_final,
        k_final,
        v_final,
        sum_qk[0],
        sum_qk[1],
        o_final,
        sums[3],
        gate_final,
        up_final,
        d_final,
    )


def solution(mesh):
    weight = P("fsdp", "tp")
    turned = P("tp", "fsdp")
    acts = P(("fsdp", "ctx"), None)
    gain = P("fsdp")
    return jax.shard_map(
        per_device,
        mesh=mesh,
        in_specs=(
            acts,
            P(("fsdp", "ctx")),
            gain,
            weight,
            weight,
            weight,
            gain,
            gain,
            turned,
            gain,
            weight,
            weight,
            turned,
            acts,
        ),
        out_specs=(
            acts,
            acts,
            gain,
            weight,
            weight,
            weight,
            gain,
            gain,
            turned,
            gain,
            weight,
            weight,
            turned,
        ),
        check_vma=False,
    )
```

profile of v0, /device:TPU:1, one launch (start us, length us, event | category | flops | bytes accessed | tf_op | source)
XLA Modules:
  0.0 292.1 jit_solution(376195433190576165)
XLA Ops:
  0.7 0.8 dynamic_slice.6
  1.4 0.7 bitcast_convert_fusion.1
  2.1 0.7 bitcast_convert_fusion
  2.7 0.1 reshape.84
  2.8 0.7 maximum_convert_fusion
  3.5 0.7 scatter.9.waves
  4.2 0.0 copy-start
  4.2 0.6 broadcast_in_dim.20.seq
  4.8 0.2 dynamic_update_slice.3.gains
  5.0 0.0 copy-start.1
  5.0 0.7 copy.28.gain_two
  5.8 0.7 copy.27.gain_one
  6.5 0.0 copy-done
  6.5 0.0 copy-done.1
  6.5 107.0 %forward.1 = (bf16[4,4,128,512]{3,2,1,0:T(8,128)(2,1)}, bf16[256,2048]{1,0:T(8,128)(2,1)}, bf16[4,4,128,1536]{3,2,1,0:T(8,128)(2,1)}, bf16[768,2048]{1,0:T(8,128...) custom-call(bf16[128,1024]{1,0:T(8,128)(2,1)} %q_weight.3, ...), custom_call_target="tpu_custom_call" | custom-call | tf_op jit(solution)/shard_map/forward/pallas_call | solution.py:581
  113.6 82.0 %middle.1 = (bf16[8,128,2048]{2,1,0:T(8,128)(2,1)}, bf16[4,4,128,1536]{3,2,1,0:T(8,128)(2,1)}, f32[128,2048]{1,0:T(8,128)}, bf16[128,2048]{1,0:T(8,128)(2,1)}, b...) custom-call(bf16[4,4,128,1536]{3,2,1,0:T(8,128)(2,1)} %get-tuple-element.78.full_gu, ...), custom_call_target="tpu_custom_call" | custom-call | tf_op jit(solution)/shard_map/middle/pallas_call | solution.py:581
  195.6 88.3 %end.1 = (bf16[2,128,2048]{2,1,0:T(8,128)(2,1)}, bf16[2,128,2048]{2,1,0:T(8,128)(2,1)}, bf16[4,128,512]{2,1,0:T(8,128)(2,1)}, bf16[4,256,128]{2,1,0:T(8,128)(2,1...) custom-call(bf16[128,1024]{1,0:T(8,128)(2,1)} %q_weight.3, ...), custom_call_target="tpu_custom_call" | custom-call | tf_op jit(solution)/shard_map/end/pallas_call | solution.py:581
  283.9 0.7 slice.45
  284.5 1.3 slice_bitcast_fusion
  285.8 0.1 constant_dynamic-slice_fusion
  285.9 0.5 slice_bitcast_fusion.1
  286.4 5.5 %widen.1 = (bf16[256,2048]{1,0:T(8,128)(2,1)}, f32[256,2048]{1,0:T(8,128)}, f32[128,1024]{1,0:T(8,128)}, f32[128,512]{1,0:T(8,128)}, f32[128,512]{1,0:T(8,128)},...) custom-call(bf16[2,128,2048]{2,1,0:T(8,128)(2,1)} %get-tuple-element.97.out_rows, ...), custom_call_target="tpu_custom_call" | custom-call | tf_op jit(solution)/shard_map/widen/pallas_call | solution.py:1656
  (4 shorter events, 0.0 us)
Async XLA Ops:
  4.2 2.3 copy-start
  5.0 1.5 copy-start.1
where the time goes:
time: 296 us; the launch traced here: 292 us
  Pallas kernels  283 us (96%)
  local copies, waits for them, and re-layouts  6.37 us (2%)
    pallas_call x3, Pallas kernels, call(): pl.pallas_call(kernel, name=name, out_shape=outs, in_specs=in_specs, out_...  277 us

commit v1 on v0

--- a/solution.py
+++ b/solution.py
@@ -1,5 +1,6 @@
 import jax
 import jax.numpy as jnp
+import numpy as np
 from jax import lax
 from jax.experimental import pallas as pl
 from jax.experimental.pallas import tpu as pltpu
@@ -386,6 +387,58 @@
         each(2 * rows, 16, body)
 
 
+class PairSum:
+    def __init__(self, links, partial, passed, cross, pair, done):
+        self.links, self.partial, self.done = links, partial, done
+        self.passed, self.cross, self.pair = passed, cross, pair
+        self.copies = {}
+
+    def over(self, y_hi):
+        core = self.links.here["core"]
+        for y in (2 * y_hi, 2 * y_hi + 1):
+            self.copies[y] = self.links.send(
+                self.partial.at[block_of(y, 1 - core)], self.passed.at[y], "core"
+            )
+
+    def ring(self):
+        links, partial, passed = self.links, self.partial, self.passed
+        core, y_hi = links.here["core"], lax.div(links.here["y"], 2)
+        rows = partial.shape[1] // 2
+        chunks = [(i, pl.ds(h * rows, rows)) for i in range(2) for h in range(2)]
+        theirs, ours = 2 - 2 * y_hi, 2 * y_hi
+        for y in range(4):
+            self.copies[y].wait_recv()
+
+        def add(first, i, w):
+            spot = passed.at[first + i, w]
+            add_rows(spot, spot, partial.at[block_of(first + i, core), w])
+
+        across = []
+        for i, w in chunks:
+            add(theirs, i, w)
+            across.append(links.send(passed.at[theirs + i, w], self.cross.at[i, w], "cross"))
+        for i, w in chunks:
+            add(ours, i, w)
+        yield
+        beside = []
+        for copy, (i, w) in zip(across, chunks):
+            copy.wait_recv()
+            spot = passed.at[ours + i, w]
+            add_rows(spot, spot, self.cross.at[i, w])
+            beside.append(links.send(spot, self.pair.at[i, w], "pair"))
+            yield
+        for n, (copy, (i, w)) in enumerate(zip(beside, chunks)):
+            copy.wait_recv()
+
+            def body(window, i=i, start=w.start):
+                at = pl.ds(pl.multiple_of(start + window.start, 16), 16)
+                self.done(i, at, full(passed[ours + i, at]) + full(self.pair[i, at]))
+
+            each(rows, 16, body)
+            if n < 3:
+                yield
+
+
 def column_scratch(rows):
     return [
         pltpu.VMEM((4, rows, 2048), LOW),
@@ -604,6 +657,12 @@
     return values * cosine + pltpu.roll(values, HD // 2, 1) * sine
 
 
+def gain_columns(gains, columns_of):
+    for i in range(2):
+        columns_of[i] = jnp.broadcast_to(gains[2 + i : 3 + i], (HD, HD)).T
+    return columns_of.at[0], columns_of.at[1]
+
+
 def forward_kernel(
     q_weight,
     k_weight,
@@ -614,8 +673,6 @@
     down_weight,
     tokens,
     cotangent,
-    gain_one,
-    gain_two,
     gains,
     seq,
     waves,
@@ -627,17 +684,23 @@
     two_all,
     dy_all,
     middle,
+    attended_out,
+    queries_out,
+    keys_out,
+    values_out,
+    proj_out,
+    table_out,
+    gains_all,
+    starts,
+    send_sems,
+    recv_sems,
+    kept,
     attended,
     queries,
     keys,
     values,
     proj,
     table,
-    gains_all,
-    starts,
-    send_sems,
-    recv_sems,
-    kept,
     raw_qkv,
     own_qkv,
     own_o,
@@ -652,6 +715,7 @@
     seq_all,
     partial,
     two_own,
+    columns_of,
     *column,
 ):
     links = Links(send_sems, recv_sems)
@@ -681,6 +745,7 @@
         local.start(down_weight.at[aligned(part * nff, nff)], down_own),
         local.start(cotangent, dy_both),
     ]
+    gain_one, gain_two = gain_columns(gains, columns_of)
     links.meet(PLANE + COLUMN)
     load_x.wait()
 
@@ -699,7 +764,7 @@
         copy.wait()
 
     def scale_qkv(window):
-        own_qkv[window] = low(full(raw_qkv[window]) * gain_one[window])
+        own_qkv[window] = low(full(raw_qkv[window]) * gain_one[window, 0:1])
         full_qkv[z, x, window] = own_qkv[window]
 
     each(own_rows, 16, scale_qkv)
@@ -714,7 +779,7 @@
         copy.wait()
 
     def scale_gu(window):
-        own_gu[window] = low(full(raw_gu[window]) * gain_two[window])
+        own_gu[window] = low(full(raw_gu[window]) * gain_two[window, 0:1])
 
     each(own_rows, 16, scale_gu)
     step_all([first_o])
@@ -841,10 +906,18 @@
             summed.over(i // 2)
         if i > 0:
             step_all([column_dy])
+    late += [
+        local.start(attended, attended_out),
+        local.start(queries, queries_out),
+        local.start(keys, keys_out),
+        local.start(values, values_out),
+        local.start(proj, proj_out),
+        local.start(table, table_out),
+    ]
     ring = summed.ring()
     step_all([ring])
+    step_all(second_late)
     step_all([ring])
-    step_all(second_late)
     together([ring])
     late.append(local.start(two_own, two_all.at[spot]))
     column_two = column_gather(links, two_own, two_all)
@@ -865,10 +938,8 @@
     middle,
     mid_all,
     grad_gu_w,
-    grad_mid,
     result,
     sum_d,
-    down_part,
     send_sems,
     recv_sems,
     kept,
@@ -950,7 +1021,6 @@
             value = middle[at]
             inverse = inverse_of(value)
             value = full(dy_own[at]) + norm_back(total, value * inverse, inverse)
-            grad_mid[at] = value
             mid_own[at] = low(value)
 
         return body
@@ -974,9 +1044,9 @@
         )
 
     sums = [column_sum(partial, column, h, done) for h in range(2)]
-    sum_down = column_sum(partial_down, column_down, 0, done_down)
+    sums_down = [column_sum(partial_down, column_down, h, done_down) for h in range(2)]
     rings = [one.ring() for one in sums]
-    ring_down = sum_down.ring()
+    rings_down = [one.ring() for one in sums_down]
     gathers = [
         column_gather(links, mid_own.at[windows[h]], mid_all.at[:, windows[h]]) for h in range(2)
     ]
@@ -995,45 +1065,50 @@
 
     units(0, 0, nff // 256)
     forward_part(0)
-    sum_down.over(0)
-    sum_down.over(1)
+    sums_down[0].over(0)
+    sums_down[0].over(1)
+    load_two[1].wait()
+    load_dy[1].wait()
+    units(1, 0, 1)
+    step_all([rings_down[0]])
+    units(1, 1, nff // 256)
+    forward_part(1)
+    sums_down[1].over(0)
+    sums_down[1].over(1)
+    step_all([rings_down[0]])
     backward_part(0, 0, 2)
-    step_all([ring_down])
+    step_all([rings_down[1]])
     backward_part(0, 2, 4)
     sums[0].over(0)
     sums[0].over(1)
-    load_two[1].wait()
-    load_dy[1].wait()
-    units(1, 0, 1)
+    backward_part(1, 0, 2)
     step_all([rings[0]])
-    units(1, 1, nff // 256)
-    step_all([ring_down, rings[0]])
-    loop(0, nff // 256, down_grad)
+    backward_part(1, 2, 4)
+    sums[1].over(0)
+    sums[1].over(1)
+    together([rings_down[0]])
+    loop(0, 1, down_grad)
+    step_all([rings[0], rings[1]])
+    loop(1, nff // 256, down_grad)
     scatter_d = plane_scatter(links, grad_d, sum_d, *plane_d)
     step_all([scatter_d])
     together([rings[0]])
     step_all([gathers[0]])
     step_all([gathers[0]])
-    backward_part(1, 0, 4)
-    sums[1].over(0)
-    sums[1].over(1)
-    together([ring_down])
     loop(0, 2, gate_up_grad)
-    step_all([rings[1], gathers[0]])
+    step_all([rings[1], rings_down[1]])
     loop(2, 4, gate_up_grad)
     keep_w = local.start(gu, grad_gu_w)
-    step_all([scatter_d, rings[1], gathers[0]])
-    forward_part(1)
-    keep_down = local.start(partial_down.at[:, windows[1]], down_part)
-    step_all([scatter_d])
+    step_all([gathers[0]])
     together([rings[1]])
     step_all([gathers[1]])
-    step_all([gathers[1]])
-    step_all([scatter_d])
+    step_all([gathers[1], scatter_d])
     keep_mid = local.start(mid_own, mid_all.at[spot])
-    step_all([gathers[1], gathers[0], scatter_d])
-    together([gathers[1], gathers[0], scatter_d])
-    for copy in (keep_w, keep_mid, keep_down):
+    together([rings_down[1]])
+    step_all([gathers[0], scatter_d])
+    step_all([gathers[1], scatter_d])
+    together([gathers[0], gathers[1], scatter_d])
+    for copy in (keep_w, keep_mid):
         copy.wait()
     links.drain()
 
@@ -1050,21 +1125,17 @@
     unit_all,
     mid_all,
     grad_gu_w,
-    attended,
-    queries,
-    keys,
-    values,
-    proj,
-    table,
+    attended_in,
+    queries_in,
+    keys_in,
+    values_in,
+    proj_in,
+    table_in,
     gains_all,
     starts,
-    gain_one,
-    gain_two,
-    grad_mid,
-    middle,
+    gains,
     result,
     sum_d,
-    down_part,
     grad_x,
     out_rows,
     all_qkv,
@@ -1075,6 +1146,13 @@
     send_sems,
     recv_sems,
     kept,
+    attended,
+    queries,
+    keys,
+    values,
+    proj,
+    table,
+    columns_of,
     weights,
     weight_o,
     unit,
@@ -1084,7 +1162,8 @@
     grad_qkv_w,
     raw_qkv,
     raw_gu,
-    x_own,
+    x_both,
+    mid_both,
     grad_att,
     dk,
     dv,
@@ -1100,12 +1179,10 @@
     row_all,
     turned,
     x_pair,
-    row_pair,
-    part_down,
     *scratch,
 ):
-    column_parts, column_down = scratch[:3], scratch[3:6]
-    plane_gu, plane_o, plane_qkv = scratch[6:11], scratch[11:16], scratch[16:]
+    passed, cross, pair = scratch[:3]
+    plane_gu, plane_o, plane_qkv = scratch[3:8], scratch[8:13], scratch[13:]
     links = Links(send_sems, recv_sems)
     local = Locals(kept)
     here = links.here
@@ -1113,18 +1190,28 @@
     half = lax.rem(y, 2)
     part = lax.div(y, 2) * 2 + core
     part_other = lax.div(lax.rem(y + 2, 4), 2) * 2 + core
-    rows, width = x_own.shape
+    _, rows, width = x_both.shape
     nq, nkv = own_o.shape[0], keys.shape[1]
     nff = sum_gu.shape[1] // 2
 
     load_mid = local.start(mid_all, mid)
     load_o = local.start(full_o, weight_o)
     load_gu = local.start(grad_gu_w, grad_gu)
-    load_down = local.start(down_part, part_down)
+    load_heads = [
+        local.start(queries_in, queries),
+        local.start(keys_in, keys),
+        local.start(values_in, values),
+        local.start(proj_in, proj),
+        local.start(table_in, table),
+        local.start(attended_in, attended),
+    ]
+    gain_one, gain_two = gain_columns(gains, columns_of)
     loads = [
         local.start(full_qkv, weights),
         local.start(unit_all, unit),
-        local.start(tokens.at[aligned(half * rows, rows)], x_own),
+        local.start(tokens.at[pl.ds(0, rows)], x_both.at[0]),
+        local.start(tokens.at[pl.ds(rows, rows)], x_both.at[1]),
+        local.start(mid_all.at[pl.ds(pl.multiple_of(2 * part, 2), 2)], mid_both),
         local.start(q_weight.at[:, aligned(part * nq, nq)], raw_qkv.at[:, pl.ds(0, nq)]),
         local.start(k_weight.at[:, aligned(part * nkv, nkv)], raw_qkv.at[:, pl.ds(nq, nkv)]),
         local.start(v_weight.at[:, aligned(part * nkv, nkv)], raw_qkv.at[:, pl.ds(nq + nkv, nkv)]),
@@ -1152,26 +1239,19 @@
         copy.wait_recv()
         keep.wait()
 
-    def done_down(window, total):
-        late = pl.ds(pl.multiple_of(rows // 2 + window.start, 16), 16)
-        row_pair[window] = result[window]
-        row_pair[late] = low(middle[late] + total)
-
-    def done_one(window, total):
-        value = full(x_own[window])
+    def done_one(i, window, total):
+        value = full(x_both[i, window])
         inverse = inverse_of(value)
-        x_pair[window] = low(grad_mid[window] + norm_back(total, value * inverse, inverse))
+        back = norm_back(total, value * inverse, inverse)
+        x_pair[i, window] = low(full(mid_both[i, window]) + back)
 
     def scale(into, total, raw, gain, spot):
         def body(window):
-            into[window] = low(full(total[window]) * gain[window])
+            into[window] = low(full(total[window]) * gain[window, 0:1])
             part_sum = jnp.sum(full(total[window]) * full(raw[window]), 1, keepdims=True)
             turned[spot, window] = jnp.broadcast_to(part_sum, (16, HD))
 
         each(rows, 16, body)
-
-    load_mid.wait()
-    load_o.wait()
 
     def attended_grad(i, carry):
         window = aligned(i * 256, 256)
@@ -1195,15 +1275,16 @@
         yield from share(own_qkv, all_qkv)
 
     job_gu, job_o, job_qkv = gu_job(), o_job(), qkv_job()
-    sum_down = ColumnSum(links, part_down, *column_down, done_down)
-    ring_down = sum_down.ring()
     share_d = share(sum_d, all_d)
+    pair_rows = exchange(result, out_rows)
+    step_all([pair_rows, share_d])
     load_gu.wait()
     step_all([job_gu])
-    load_down.wait()
-    sum_down.over(0)
-    sum_down.over(1)
+    load_mid.wait()
+    load_o.wait()
     lax.fori_loop(0, 4, attended_grad, 0)
+    for copy in load_heads:
+        copy.wait()
 
     gain_rows = jnp.sum(gains_all[...], (0, 1))
     q_gain, k_gain = gain_rows[0:1], gain_rows[1:2]
@@ -1248,10 +1329,8 @@
             grad_qkv[window, head * HD : (head + 1) * HD] = project_back(
                 dq[head * 256 : (head + 1) * 256], head, window, q_gain
             )
-        if i == 0:
-            step_all([ring_down])
-        if i == 2:
-            step_all([ring_down, share_d])
+        if i == 3:
+            step_all([share_d])
 
     def keys_back(i, carry):
         window = aligned(i * 256, 256)
@@ -1274,12 +1353,9 @@
 
     for copy in loads:
         copy.wait()
-    sum_one = ColumnSum(links, mid, *column_parts, done_one)
+    sum_one = PairSum(links, mid, passed, cross, pair, done_one)
     grad_o[...] = low(dot_tn(attended[...], mid[...].reshape(8 * rows, width)))
     step_all([job_o])
-    together([ring_down])
-    pair_rows = exchange(row_pair, out_rows)
-    step_all([pair_rows])
     lax.fori_loop(0, 2, unit_grad, 0)
     sum_one.over(0)
     lax.fori_loop(2, 4, unit_grad, 0)
@@ -1295,23 +1371,29 @@
         return carry
 
     lax.fori_loop(0, 4, weight_grad, 0)
-    step_all([job_qkv, job_gu, job_o, small_job])
-    step_all([share_d, job_o])
+    step_all([job_qkv])
     step_all([ring_one])
-    step_all([job_gu, job_qkv, job_o])
-    step_all([job_gu, job_qkv, small_job])
-    together([ring_one])
-    pair_x = exchange(x_pair, grad_x)
-    step_all([pair_x, job_gu, job_qkv])
+    step_all([job_o, small_job])
+    step_all([ring_one])
     step_all([job_gu, job_qkv])
+    step_all([ring_one])
+    step_all([job_o, job_qkv, share_d])
+    step_all([ring_one])
+    step_all([job_gu, job_o, job_qkv])
+    for _ in range(3):
+        step_all([ring_one])
+    step_all([job_gu, job_o, job_qkv])
+    together([small_job])
     row[0:2] = jnp.sum(small_all[:, :, 0:2], (0, 1))
     row[2:3] = turned[0].T[0:1]
     row[3:4] = turned[1].T[0:1]
     row[4:8] = jnp.zeros((4, HD), WIDE)
     row_job = small_column(links, row, row_all)
-    step_all([row_job, job_o, job_gu, job_qkv])
-    together([job_o, job_gu, job_qkv, row_job, share_d, pair_rows])
-    together([pair_x])
+    step_all([row_job])
+    together([ring_one])
+    keep_x = local.start(x_pair, grad_x)
+    together([row_job, job_o, job_gu, job_qkv, share_d, pair_rows])
+    keep_x.wait()
     sums_out[...] = jnp.sum(row_all[...], (0, 1))
     links.drain()
 
@@ -1429,22 +1511,24 @@
     def own(array):
         return lax.dynamic_slice_in_dim(array, half * own_rows, own_rows, 0)
 
-    attn_gain_f = jnp.broadcast_to(full(attn_gain)[:, None], (attn_gain.shape[0], 1))
-    mlp_gain_f = jnp.broadcast_to(full(mlp_gain)[:, None], (mlp_gain.shape[0], 1))
     rows_w = q_weight.shape[0]
     nq, nkv, nff = q_weight.shape[1] // parts, k_weight.shape[1] // parts, gate_weight.shape[1] // parts
     na, nb = nq + 2 * nkv, 2 * nff
     few = q_gain.shape[0]
-    gains = lax.dynamic_update_slice(
-        jnp.zeros((8, HD), WIDE),
+    spread = lax.dynamic_update_slice(
+        jnp.zeros((2, HD), WIDE),
         full(jnp.stack([q_gain, k_gain])),
         (0, lax.axis_index("fsdp") * few),
     )
+    gains = jnp.concatenate(
+        [spread, full(attn_gain)[None], full(mlp_gain)[None], jnp.zeros((4, HD), WIDE)], 0
+    )
     seq = jnp.broadcast_to(own(segments)[None, :], (8, own_rows))
-    frequency = jnp.power(rope_base, -2.0 * jnp.arange(HD // 2, dtype=WIDE) / HD)
-    ones = jnp.ones((HD // 2,), WIDE)
-    waves = jnp.zeros((8, HD), WIDE).at[0].set(jnp.tile(frequency, 2))
-    waves = waves.at[1].set(jnp.concatenate([-ones, ones]))
+    index = np.arange(HD)
+    frequency = np.power(rope_base, -2.0 * (index % (HD // 2)) / HD)
+    waves = np.zeros((8, HD), np.float32)
+    waves[0] = frequency
+    waves[1] = np.where(index < HD // 2, -1.0, 1.0)
 
     (
         full_qkv,
@@ -1487,9 +1571,15 @@
             shaped((4, 4, 8, HD), WIDE),
             shaped((8, HD), WIDE),
         ),
-        [HBM] * 7 + [VMEM] * 9,
-        [HBM] * 9 + [VMEM] * 5,
+        [HBM] * 7 + [VMEM] + [HBM] * 6 + [VMEM] * 2,
+        [HBM] * 9 + [VMEM] * 3,
         [
+            pltpu.VMEM((seq_len, nq), LOW),
+            pltpu.VMEM((2, seq_len, HD), LOW),
+            pltpu.VMEM((seq_len, HD), LOW),
+            pltpu.VMEM((seq_len, HD), LOW),
+            pltpu.VMEM((3, seq_len, HD), WIDE),
+            pltpu.VMEM((2, seq_len, HD), WIDE),
             pltpu.VMEM((rows_w, na), LOW),
             pltpu.VMEM((rows_w, na), LOW),
             pltpu.VMEM((nq, rows_w), LOW),
@@ -1504,6 +1594,7 @@
             pltpu.VMEM((2, 4, 8, own_rows), jnp.int32),
             pltpu.VMEM((blocks, own_rows, width), LOW),
             pltpu.VMEM((own_rows, width), LOW),
+            pltpu.VMEM((2, HD, HD), WIDE),
         ]
         + column_scratch(own_rows),
         58,
@@ -1517,15 +1608,13 @@
             down_weight,
             tokens,
             cotangent,
-            attn_gain_f,
-            mlp_gain_f,
             gains,
             seq,
-            waves,
+            jnp.asarray(waves),
         ),
     )
 
-    mid_all, grad_gu_w, grad_mid, result, sum_d, down_part = call(
+    mid_all, grad_gu_w, result, sum_d = call(
         middle_kernel,
         "middle",
         1,
@@ -1534,12 +1623,10 @@
         (
             shaped((blocks, own_rows, width)),
             shaped((4, 4, rows_w, nb)),
-            shaped((own_rows, width), WIDE),
             shaped((own_rows, width)),
             shaped((nff, rows_w)),
-            shaped((blocks, own_rows // 2, width)),
         ),
-        [HBM] * 2 + [VMEM] * 3 + [HBM],
+        [HBM] * 2 + [VMEM] * 2,
         [HBM] * 4 + [VMEM],
         [
             pltpu.VMEM((4, 4, rows_w, nb), LOW),
@@ -1555,7 +1642,7 @@
             pltpu.VMEM((own_rows, width), LOW),
         ]
         + column_scratch(own_rows)
-        + column_scratch(own_rows // 2)
+        + column_scratch(own_rows)
         + plane_scratch(nff // 2, rows_w),
         62,
         (full_gu, full_d, two_all, dy_all, middle),
@@ -1577,8 +1664,15 @@
             shaped((8, HD), WIDE),
         ),
         [HBM] * 6 + [VMEM],
-        [HBM] * 11 + [VMEM] * 14 + [HBM],
+        [HBM] * 17 + [VMEM] * 5,
         [
+            pltpu.VMEM((seq_len, nq), LOW),
+            pltpu.VMEM((2, seq_len, HD), LOW),
+            pltpu.VMEM((seq_len, HD), LOW),
+            pltpu.VMEM((seq_len, HD), LOW),
+            pltpu.VMEM((3, seq_len, HD), WIDE),
+            pltpu.VMEM((2, seq_len, HD), WIDE),
+            pltpu.VMEM((2, HD, HD), WIDE),
             pltpu.VMEM((4, 4, rows_w, na), LOW),
             pltpu.VMEM((nq, width), LOW),
             pltpu.VMEM((blocks, own_rows, width), LOW),
@@ -1588,7 +1682,8 @@
             pltpu.VMEM((4, 4, rows_w, na), LOW),
             pltpu.VMEM((rows_w, na), LOW),
             pltpu.VMEM((rows_w, nb), LOW),
-            pltpu.VMEM((own_rows, width), LOW),
+            pltpu.VMEM((halves, own_rows, width), LOW),
+            pltpu.VMEM((halves, own_rows, width), LOW),
             pltpu.VMEM((2, seq_len, HD), LOW),
             pltpu.VMEM((seq_len, HD), WIDE),
             pltpu.VMEM((seq_len, HD), WIDE),
@@ -1603,12 +1698,11 @@
             pltpu.VMEM((8, HD), WIDE),
             pltpu.VMEM((2, 4, 8, HD), WIDE),
             pltpu.VMEM((2, rows_w, HD), WIDE),
-            pltpu.VMEM((own_rows, width), LOW),
-            pltpu.VMEM((own_rows, width), LOW),
-            pltpu.VMEM((blocks, own_rows // 2, width), LOW),
+            pltpu.VMEM((halves, own_rows, width), LOW),
+            pltpu.VMEM((4, own_rows, width), LOW),
+            pltpu.VMEM((halves, own_rows, width), LOW),
+            pltpu.VMEM((halves, own_rows, width), LOW),
         ]
-        + column_scratch(own_rows)
-        + column_scratch(own_rows // 2)
         + plane_scratch(rows_w, nb // 2)
         + plane_scratch(nq // 2, rows_w)
         + plane_scratch(rows_w, na // 2),
@@ -1633,13 +1727,9 @@
             table,
             gains_all,
             starts,
-            attn_gain_f,
-            mlp_gain_f,
-            grad_mid,
-            middle,
+            gains,
             result,
             sum_d,
-            down_part,
         ),
     )
 

time: 296 us -> 302 us (1.020)
  Pallas kernels: 283 us -> 291 us
    pallas_call x3, Pallas kernels: 277 us -> 285 us  [call(): pl.pallas_call(kernel, name=name, out_shape=outs, in_specs=in_specs, out_...]
where the time goes in v1:
time: 302 us; the launch traced here: 298 us
  Pallas kernels  291 us (96%)
  local copies, waits for them, and re-layouts  4.13 us (1%)
    pallas_call x3, Pallas kernels, call(): pl.pallas_call(kernel, name=name, out_shape=outs, in_specs=in_specs, out_...  285 us

profile of v1, /device:TPU:1, one launch (start us, length us, event | category | flops | bytes accessed | tf_op | source)
XLA Modules:
  0.0 297.9 jit_solution(1447850729236760050)
XLA Ops:
  0.7 0.8 dynamic_slice.6
  1.4 0.1 pad.3.clone
  1.5 0.7 maximum_convert_fusion
  2.2 0.1 dynamic_update_slice.3
  2.3 0.7 bitcast_convert_fusion
  3.0 0.7 maximum_maximum_fusion.gains
  3.7 0.6 broadcast_in_dim.30.seq
  4.3 105.0 %forward.1 = (bf16[4,4,128,512]{3,2,1,0:T(8,128)(2,1)}, bf16[256,2048]{1,0:T(8,128)(2,1)}, bf16[4,4,128,1536]{3,2,1,0:T(8,128)(2,1)}, bf16[768,2048]{1,0:T(8,128...) custom-call(bf16[128,1024]{1,0:T(8,128)(2,1)} %q_weight.3, ...), custom_call_target="tpu_custom_call" | custom-call | tf_op jit(solution)/shard_map/forward/pallas_call | solution.py:634
  109.3 93.7 %middle.1 = (bf16[8,128,2048]{2,1,0:T(8,128)(2,1)}, bf16[4,4,128,1536]{3,2,1,0:T(8,128)(2,1)}, bf16[128,2048]{1,0:T(8,128)(2,1)}, bf16[768,128]{1,0:T(8,128)(2,1)}) custom-call(bf16[4,4,128,1536]{3,2,1,0:T(8,128)(2,1)} %get-tuple-element.52.full_gu, bf16[768,2048]{1,0:T(8,128)(2,1)} %get-tuple-element.53.full_d, ...), custom_call_target="tpu_custom_call" | custom-call | tf_op jit(solution)/shard_map/middle/pallas_call | solution.py:634
  202.9 86.7 %end.1 = (bf16[2,128,2048]{2,1,0:T(8,128)(2,1)}, bf16[2,128,2048]{2,1,0:T(8,128)(2,1)}, bf16[4,128,512]{2,1,0:T(8,128)(2,1)}, bf16[4,256,128]{2,1,0:T(8,128)(2,1...) custom-call(bf16[128,1024]{1,0:T(8,128)(2,1)} %q_weight.3, ...), custom_call_target="tpu_custom_call" | custom-call | tf_op jit(solution)/shard_map/end/pallas_call | solution.py:634
  289.6 0.7 slice.16
  290.3 1.3 slice_bitcast_fusion
  291.6 0.1 constant_dynamic-slice_fusion
  291.7 0.5 slice_bitcast_fusion.1
  292.2 5.5 %widen.1 = (bf16[256,2048]{1,0:T(8,128)(2,1)}, f32[256,2048]{1,0:T(8,128)}, f32[128,1024]{1,0:T(8,128)}, f32[128,512]{1,0:T(8,128)}, f32[128,512]{1,0:T(8,128)},...) custom-call(bf16[2,128,2048]{2,1,0:T(8,128)(2,1)} %get-tuple-element.69.out_rows, ...), custom_call_target="tpu_custom_call" | custom-call | tf_op jit(solution)/shard_map/widen/pallas_call | solution.py:1746
  (2 shorter events, 0.0 us)

commit v2 on v1

--- a/solution.py
+++ b/solution.py
@@ -1,6 +1,5 @@
 import jax
 import jax.numpy as jnp
-import numpy as np
 from jax import lax
 from jax.experimental import pallas as pl
 from jax.experimental.pallas import tpu as pltpu
@@ -1524,11 +1523,11 @@
         [spread, full(attn_gain)[None], full(mlp_gain)[None], jnp.zeros((4, HD), WIDE)], 0
     )
     seq = jnp.broadcast_to(own(segments)[None, :], (8, own_rows))
-    index = np.arange(HD)
-    frequency = np.power(rope_base, -2.0 * (index % (HD // 2)) / HD)
-    waves = np.zeros((8, HD), np.float32)
-    waves[0] = frequency
-    waves[1] = np.where(index < HD // 2, -1.0, 1.0)
+    index = lax.broadcasted_iota(WIDE, (8, HD), 1)
+    row = lax.broadcasted_iota(WIDE, (8, HD), 0)
+    lower = index < HD // 2
+    frequency = jnp.power(rope_base, -2.0 * jnp.where(lower, index, index - HD // 2) / HD)
+    waves = jnp.where(row == 0, frequency, jnp.where(lower, -1.0, 1.0))
 
     (
         full_qkv,
@@ -1610,7 +1609,7 @@
             cotangent,
             gains,
             seq,
-            jnp.asarray(waves),
+            waves,
         ),
     )
 

time: 302 us -> 302 us (level)
  no operation moved by 1% of the time
where the time goes in v2:
time: 302 us; the launch traced here: 299 us
  Pallas kernels  291 us (96%)
  local copies, waits for them, and re-layouts  4.11 us (1%)
    pallas_call x3, Pallas kernels, call(): pl.pallas_call(kernel, name=name, out_shape=outs, in_specs=in_specs, out_...  285 us

profile of v2, /device:TPU:1, one launch (start us, length us, event | category | flops | bytes accessed | tf_op | source)
XLA Modules:
  0.0 298.5 jit_solution(10774469129871327439)
XLA Ops:
  0.7 0.8 dynamic_slice.6
  1.4 0.1 pad.3.clone
  1.5 0.7 maximum_convert_fusion
  2.2 0.1 dynamic_update_slice.3
  2.3 0.7 bitcast_convert_fusion
  3.0 0.7 maximum_maximum_fusion.gains
  3.7 0.7 power_select_fusion.waves
  4.4 0.6 broadcast_in_dim.38.seq
  4.9 105.0 %forward.1 = (bf16[4,4,128,512]{3,2,1,0:T(8,128)(2,1)}, bf16[256,2048]{1,0:T(8,128)(2,1)}, bf16[4,4,128,1536]{3,2,1,0:T(8,128)(2,1)}, bf16[768,2048]{1,0:T(8,128...) custom-call(bf16[128,1024]{1,0:T(8,128)(2,1)} %q_weight.3, ...), custom_call_target="tpu_custom_call" | custom-call | tf_op jit(solution)/shard_map/forward/pallas_call | solution.py:633
  109.9 93.7 %middle.1 = (bf16[8,128,2048]{2,1,0:T(8,128)(2,1)}, bf16[4,4,128,1536]{3,2,1,0:T(8,128)(2,1)}, bf16[128,2048]{1,0:T(8,128)(2,1)}, bf16[768,128]{1,0:T(8,128)(2,1)}) custom-call(bf16[4,4,128,1536]{3,2,1,0:T(8,128)(2,1)} %get-tuple-element.52.full_gu, bf16[768,2048]{1,0:T(8,128)(2,1)} %get-tuple-element.53.full_d, ...), custom_call_target="tpu_custom_call" | custom-call | tf_op jit(solution)/shard_map/middle/pallas_call | solution.py:633
  203.6 86.7 %end.1 = (bf16[2,128,2048]{2,1,0:T(8,128)(2,1)}, bf16[2,128,2048]{2,1,0:T(8,128)(2,1)}, bf16[4,128,512]{2,1,0:T(8,128)(2,1)}, bf16[4,256,128]{2,1,0:T(8,128)(2,1...) custom-call(bf16[128,1024]{1,0:T(8,128)(2,1)} %q_weight.3, ...), custom_call_target="tpu_custom_call" | custom-call | tf_op jit(solution)/shard_map/end/pallas_call | solution.py:633
  290.3 0.7 slice.16
  291.0 1.3 slice_bitcast_fusion
  292.2 0.1 constant_dynamic-slice_fusion
  292.3 0.5 slice_bitcast_fusion.1
  292.8 5.5 %widen.1 = (bf16[256,2048]{1,0:T(8,128)(2,1)}, f32[256,2048]{1,0:T(8,128)}, f32[128,1024]{1,0:T(8,128)}, f32[128,512]{1,0:T(8,128)}, f32[128,512]{1,0:T(8,128)},...) custom-call(bf16[2,128,2048]{2,1,0:T(8,128)(2,1)} %get-tuple-element.69.out_rows, ...), custom_call_target="tpu_custom_call" | custom-call | tf_op jit(solution)/shard_map/widen/pallas_call | solution.py:1745
  (5 shorter events, 0.0 us)
